TPU v7x, 32 devices: a whole 2x2x4 slice. The times are simulated.
32 devices in a mesh: ctx: 16 (over z, y, core), tp: 2 (over x).
Axes of the slice: x: 2, y: 2, z: 4, core: 2. Of those that a mesh axis runs over, the one named last changes fastest.
Arguments:
- queries: bfloat16 [2048, 2048], P('ctx', 'tp'), may hold values from -200 to 200, as said below
- key_rows: bfloat16 [2048, 256], P('ctx', 'tp'), may hold values from -6 to 6
- value_rows: bfloat16 [2048, 256], P('ctx', 'tp'), may hold values from -6 to 6
- retained: int32 [16, 2, 16], P('ctx', 'tp'), may hold values from 0 to 127, as said below
Outputs:
- context: bfloat16 [2048, 2048], P(('ctx', 'tp'))
Inputs may be any that keep to these rules, and one draw needn't show every extreme that they name: `queries`: queries of order one; some rows may be large multiples of earlier keys. `retained`: each list holds 16 different row numbers of its block in increasing order, always the first row 0 and the last row 127.
All inputs are finite; a program needn't handle non-finite values.
Results may differ from a plain program's by a relative error of at most 0.0033.
Values may be sent and summed in bfloat16 or wider, within the bound.
A program may use at most 64 MiB of HBM per device.

v0:
```python
import math

import jax
import jax.numpy as jnp
from jax import lax
from jax.sharding import PartitionSpec as P

key_tile = 512


def from_root(block, axis, holder):
    block = jnp.where(lax.axis_index(axis) == holder, block, jnp.zeros_like(block))
    return lax.psum(block, axis)


def fold_block(state_now, query_heads, key_block, value_block, visible, scale_factor):
    running_max, running_sum, running_acc = state_now
    block_scores = (
        jnp.einsum("bjd,kd->bjk", query_heads, key_block, preferred_element_type=jnp.float32)
        * scale_factor
    )
    block_scores = jnp.where(visible[None, None, :], block_scores, -jnp.inf)
    new_max = jnp.maximum(running_max, jnp.max(block_scores, axis=-1))
    shrink = jnp.exp(running_max - new_max)
    weights = jnp.exp(block_scores - new_max[..., None])
    new_sum = running_sum * shrink + jnp.sum(weights, axis=-1)
    new_acc = running_acc * shrink[..., None] + jnp.einsum(
        "bjk,kd->bjd", weights.astype(jnp.bfloat16), value_block, preferred_element_type=jnp.float32
    )
    return (new_max, new_sum, new_acc)


def fold_rows(state_now, query_heads, key_block, value_block, visible, scale_factor):
    total_rows = key_block.shape[0]
    for row_begin in range(0, total_rows, key_tile):
        row_end = min(row_begin + key_tile, total_rows)
        state_now = fold_block(
            state_now,
            query_heads,
            key_block[row_begin:row_end],
            value_block[row_begin:row_end],
            visible[row_begin:row_end],
            scale_factor,
        )
    return state_now


def shards(queries, key_rows, value_rows, retained):
    row_count = queries.shape[0]
    head_size = key_rows.shape[1]
    group_size = queries.shape[1] // head_size
    keep_rows = retained.shape[2]
    scale_factor = 1.0 / math.sqrt(head_size)
    query_heads = queries.reshape(row_count, group_size, head_size)
    host_index = lax.axis_index("ctx")
    picks = retained[0, 0]
    kept_keys = jnp.take(key_rows, picks, axis=0)
    kept_values = jnp.take(value_rows, picks, axis=0)
    anchor_pair = from_root(jnp.stack([key_rows, value_rows]), "ctx", 0)
    positions = jnp.arange(row_count, dtype=jnp.int32)
    causal = positions[None, :] <= positions[:, None]
    local_scores = (
        jnp.einsum("bjd,kd->bjk", query_heads, key_rows, preferred_element_type=jnp.float32)
        * scale_factor
    )
    local_scores = jnp.where(causal[:, None, :], local_scores, -jnp.inf)
    local_max = jnp.max(local_scores, axis=-1)
    local_weights = jnp.exp(local_scores - local_max[..., None])
    state_now = (
        local_max,
        jnp.sum(local_weights, axis=-1),
        jnp.einsum(
            "bjk,kd->bjd",
            local_weights.astype(jnp.bfloat16),
            value_rows,
            preferred_element_type=jnp.float32,
        ),
    )
    anchor_visible = jnp.broadcast_to(host_index > 0, (row_count,))
    state_now = fold_rows(
        state_now, query_heads, anchor_pair[0], anchor_pair[1], anchor_visible, scale_factor
    )
    piece_keys = lax.all_gather(kept_keys, "ctx", axis=0, tiled=True)
    piece_values = lax.all_gather(kept_values, "ctx", axis=0, tiled=True)
    count = piece_keys.shape[0]
    owners = jnp.arange(count, dtype=jnp.int32) // keep_rows
    visible = (owners >= 1) & (owners < host_index)
    state_now = fold_rows(state_now, query_heads, piece_keys, piece_values, visible, scale_factor)
    result = (state_now[2] / state_now[1][..., None]).astype(jnp.bfloat16)
    result = result.reshape(row_count, group_size * head_size)
    return lax.all_to_all(result, "tp", split_axis=0, concat_axis=1, tiled=True)


def solution(mesh):
    in_specs = (P("ctx", "tp"), P("ctx", "tp"), P("ctx", "tp"), P("ctx", "tp", None))
    out_specs = P(("ctx", "tp"), None)
    return jax.shard_map(shards, mesh=mesh, in_specs=in_specs, out_specs=out_specs, check_vma=False)
```

profile of v0, /device:TPU:8, one launch (start us, length us, event | category | flops | bytes accessed | tf_op | source)
XLA Modules:
  0.0 117.5 jit_solution(16325479169253966194)
XLA Ops:
  6.5 0.0 copy-start
  6.5 0.0 all-reduce.2.cloned.1.call-start
  6.5 1.5 %maximum_select_fusion = bf16[2,128,128]{2,1,0:T(8,128)(2,1)} fusion(bf16[1,128,128]{2,1,0:T(8,128)(2,1)} %bitcast.63, bf16[1,128,128]{2,1,0:T(8,128)(2,1)} %bitcast.64, pred[]{:T(512)S(6)} %eq.3), kind=kLoop, calls=%fused_computation.34 | loop fusion | flops 65536 | bytes 131073 | tf_op jit(solution)/shard_map/jit(_where)/select_n | solution.py:12
  8.0 0.0 copy-start.4
  8.0 0.0 copy-start.2
  8.0 0.0 all-reduce.2.cloned.1.call-update
  8.0 0.6 copy-done.4
  8.7 0.0 copy-start.1
  8.7 0.1 copy-done.2
  8.8 0.6 gather_fusion
  9.3 0.1 copy-done.1
  9.4 0.6 gather_fusion.1
  10.0 0.1 broadcast_select_fusion
  10.1 19.0 %all_gather.6 = bf16[256,128]{1,0:T(8,128)(2,1)S(1)} all-gather(bf16[16,128]{1,0:T(8,128)(2,1)S(1)} %get-tuple-element.12), channel_id=1, replica_groups=mesh['ctx'=16,'tp'=2] {'ctx'}, dimensions={0}, use_global_device_ids=true | all-gather | bytes 69632 | tf_op jit(solution)/shard_map/all_gather | solution.py:83
  29.1 0.0 copy-done
  29.1 0.3 fusion.31
  29.4 0.2 fusion.32
  29.7 17.6 %all_gather.7 = bf16[256,128]{1,0:T(8,128)(2,1)S(1)} all-gather(bf16[16,128]{1,0:T(8,128)(2,1)S(1)} %get-tuple-element.11), channel_id=1, replica_groups=mesh['ctx'=16,'tp'=2] {'ctx'}, dimensions={0}, use_global_device_ids=true | all-gather | bytes 69632 | tf_op jit(solution)/shard_map/all_gather | solution.py:84
  47.3 51.8 %all-reduce.2.cloned.1.call-done = bf16[2,128,128]{2,1,0:T(8,128)(2,1)} async-done(((bf16[2,128,128]{2,1,0:T(8,128)(2,1)}), bf16[2,128,128]{2,1,0:T(8,128)(2,1)}) %all-reduce.2.cloned.1.call-update) | async-done | bytes 65552 | tf_op jit(solution)/shard_map/psum | solution.py:13
  99.0 1.0 fusion.33
  100.1 0.2 fusion.8
  100.2 0.2 fusion.12
  100.4 0.0 copy-start.3
  100.4 0.3 convolution_multiply_fusion.2
  100.7 0.5 copy-done.3
  101.3 0.3 fusion.6
  101.6 0.4 fusion.7
  102.0 0.2 copy.24
  102.1 0.1 all_to_all.14
  102.3 7.7 %all_to_all.19 = bf16[2,64,1024]{2,1,0:T(8,128)(2,1)S(1)} all-to-all(bf16[2,64,1024]{2,1,0:T(8,128)(2,1)S(1)} %all_to_all.14), channel_id=1, replica_groups=mesh['ctx'=16,'tp'=2] {'tp'}, dimensions={0} | all-to-all | bytes 524288 | tf_op jit(solution)/shard_map/all_to_all | solution.py:91
  110.0 0.7 copy.30
  (7 shorter events, 0.1 us)
Async XLA Ops:
  6.5 22.6 %copy-start = (bf16[128,1024]{1,0:T(8,128)(2,1)S(1)}, bf16[128,1024]{1,0:T(8,128)(2,1)}, u32[]{:S(2)}) copy-start(bf16[128,1024]{1,0:T(8,128)(2,1)} %param.6) | copy-start | bytes 786436
  6.5 92.5 %all-reduce.2.cloned.1.call-start = ((), (), s32[]{:S(2)}) async-start(), calls=%async_computation.1 | async-start | bytes 131072 | tf_op jit(solution)/shard_map/psum | solution.py:13
  8.0 0.7 copy-start.4
  8.0 0.8 copy-start.2
  8.7 0.8 copy-start.1
  100.4 0.8 copy-start.3
Sparse Core Ops, SparseCore 0:
  10.8 88.1 all-reduce.1
where the time goes:
time: 118 us
  waiting for transfers between devices  51.8 us (44%)
  blocking collectives  44.3 us (38%)
  between operations  13.5 us (11%)
  local copies, waits for them, and re-layouts  3.48 us (3%)
  matrix products  2.55 us (2%)
  other arithmetic  1.91 us (2%)
    psum x1, waiting for transfers between devices, from_root(): return lax.psum(block, axis)  51.8 us
    all_gather x1, blocking collectives, shards(): piece_keys = lax.all_gather(kept_keys, 'ctx', axis=0, tiled=True)  19 us
    all_gather x1, blocking collectives, shards(): piece_values = lax.all_gather(kept_values, 'ctx', axis=0, tiled=True)  17.6 us
    all_to_all x1, blocking collectives, shards(): return lax.all_to_all(result, 'tp', split_axis=0, concat_axis=1, tiled=True)  7.71 us
  transfers between devices with their start and end apart: 1, of which 1 were waited for; matrix products, arithmetic and copies ran while one was open for 2% of the time, Pallas kernels for 0%

commit v1 on v0

v1 whole, which is shorter than its diff:
```python
import functools
import math

import jax
import jax.numpy as jnp
from jax import lax
from jax.experimental import pallas as pl
from jax.experimental.pallas import tpu as pltpu
from jax.sharding import PartitionSpec as P

MESH = pl.DeviceIdType.MESH
heads_per_step = 2


def kernel(
    n, tps, far, q_hbm, k_hbm, v_hbm, pick_hbm, out,
    q, kv, kept, picks, local_scores, stage,
    load_sem, kv_send, kv_recv, out_send, out_recv, own_sem,
):
    rows, width = q_hbm.shape
    hd = k_hbm.shape[1]
    keep = picks.shape[2]
    group = width // hd
    part = rows // tps
    steps = group // heads_per_step
    h = lax.axis_index("ctx")
    t = lax.axis_index("tp")
    scale = math.log2(math.e) / math.sqrt(hd)

    loads = [
        pltpu.make_async_copy(k_hbm, kv.at[pl.ds(far, rows), pl.ds(0, hd)], load_sem.at[0]),
        pltpu.make_async_copy(v_hbm, kv.at[pl.ds(far, rows), pl.ds(hd, hd)], load_sem.at[1]),
        pltpu.make_async_copy(pick_hbm, picks, load_sem.at[2]),
        pltpu.make_async_copy(q_hbm, q, load_sem.at[3]),
    ]
    for load in loads:
        load.start()
    kv[0:far, 0 : 2 * hd] = jnp.zeros((far, 2 * hd), kv.dtype)
    kv[:, 2 * hd :] = jnp.ones((far + rows, hd), kv.dtype)

    barrier = pltpu.get_barrier_semaphore()

    def greet(j, carry):
        pl.semaphore_signal(barrier, inc=1, device_id={"ctx": j}, device_id_type=MESH)
        return carry

    lax.fori_loop(0, h, greet, 0)
    for d in range(1, tps):
        pl.semaphore_signal(
            barrier, inc=1, device_id={"tp": lax.rem(t + d, tps)}, device_id_type=MESH
        )

    loads[0].wait()
    loads[1].wait()
    loads[2].wait()
    hit = lax.broadcasted_iota(jnp.int32, (rows, keep), 0) == picks[0]
    kept[...] = lax.dot_general(
        hit.astype(jnp.float32).astype(jnp.bfloat16),
        kv[far:, 0 : 2 * hd],
        (((0,), (0,)), ((), ())),
        preferred_element_type=jnp.float32,
    ).astype(kept.dtype)

    pl.semaphore_wait(barrier, (n - 1 - h) + (tps - 1))

    def anchor_copy(j):
        return pltpu.make_async_remote_copy(
            src_ref=kv.at[pl.ds(far, rows), pl.ds(0, 2 * hd)],
            dst_ref=kv.at[pl.ds(0, rows), pl.ds(0, 2 * hd)],
            send_sem=kv_send.at[j],
            recv_sem=kv_recv.at[0],
            device_id={"ctx": j},
            device_id_type=MESH,
        )

    def kept_copy(owner, j):
        return pltpu.make_async_remote_copy(
            src_ref=kept,
            dst_ref=kv.at[pl.ds(rows + keep * (owner - 1), keep), pl.ds(0, 2 * hd)],
            send_sem=kv_send.at[j],
            recv_sem=kv_recv.at[owner],
            device_id={"ctx": j},
            device_id_type=MESH,
        )

    @pl.when(h == 0)
    def _():
        def go(i, carry):
            anchor_copy(n - i).start()
            return carry

        lax.fori_loop(1, n, go, 0)

    @pl.when(h > 0)
    def _():
        def go(j, carry):
            kept_copy(h, j).start()
            return carry

        lax.fori_loop(h + 1, n, go, 0)

    loads[3].wait()
    high = heads_per_step * rows
    causal = lax.broadcasted_iota(jnp.int32, (rows, rows), 1) <= lax.broadcasted_iota(
        jnp.int32, (rows, rows), 0
    )
    near = jnp.where(causal, 0.0, -jnp.inf)
    near = jnp.concatenate([near] * heads_per_step, axis=0)

    def head_rows(step):
        return jnp.concatenate(
            [
                q[:, (step * heads_per_step + i) * hd : (step * heads_per_step + i + 1) * hd]
                for i in range(heads_per_step)
            ],
            axis=0,
        )

    contract = (((1,), (1,)), ((), ()))
    for step in range(steps):
        local_scores[step * high : (step + 1) * high, :] = (
            lax.dot_general(
                head_rows(step), kv[far:, 0:hd], contract, preferred_element_type=jnp.float32
            )
            + near
        )

    @pl.when(h > 0)
    def _():
        anchor_copy(0).wait_recv()

        def arrive(j, carry):
            kept_copy(j, 0).wait_recv()
            return carry

        lax.fori_loop(1, h, arrive, 0)

    limit = jnp.where(h > 0, rows + keep * (h - 1), 0)
    bias = jnp.where(lax.broadcasted_iota(jnp.int32, (1, far), 1) < limit, 0.0, -jnp.inf)

    def out_copy(step, target, source):
        wide = heads_per_step * hd
        return pltpu.make_async_remote_copy(
            src_ref=stage.at[pl.ds(pl.multiple_of(target * part, part), part), pl.ds(step * wide, wide)],
            dst_ref=out.at[:, pl.ds(pl.multiple_of(source * width + step * wide, wide), wide)],
            send_sem=out_send.at[target, step],
            recv_sem=out_recv.at[source, step],
            device_id={"tp": target},
            device_id_type=MESH,
        )

    def own_copy(step):
        wide = heads_per_step * hd
        return pltpu.make_async_copy(
            stage.at[pl.ds(pl.multiple_of(t * part, part), part), pl.ds(step * wide, wide)],
            out.at[:, pl.ds(pl.multiple_of(t * width + step * wide, wide), wide)],
            own_sem.at[step],
        )

    for step in range(steps):
        scores = (
            lax.dot_general(
                head_rows(step), kv[0:far, 0:hd], contract, preferred_element_type=jnp.float32
            )
            + bias
        )
        own = local_scores[step * high : (step + 1) * high, :]
        top = jnp.maximum(
            jnp.max(scores, axis=1, keepdims=True), jnp.max(own, axis=1, keepdims=True)
        )
        weights = jnp.concatenate(
            [
                jnp.exp2((scores - top) * scale).astype(jnp.bfloat16),
                jnp.exp2((own - top) * scale).astype(jnp.bfloat16),
            ],
            axis=1,
        )
        summed = jnp.dot(weights, kv[:, hd:], preferred_element_type=jnp.float32)
        result = (summed[:, 0:hd] / summed[:, hd:]).astype(stage.dtype)
        for i in range(heads_per_step):
            head = step * heads_per_step + i
            stage[:, head * hd : (head + 1) * hd] = result[i * rows : (i + 1) * rows]
        for d in range(1, tps):
            out_copy(step, lax.rem(t + d, tps), t).start()
        own_copy(step).start()

    for step in range(steps):
        own_copy(step).wait()
        for d in range(1, tps):
            other = lax.rem(t + d, tps)
            out_copy(step, other, t).wait_send()
            out_copy(step, other, other).wait_recv()

    @pl.when(h == 0)
    def _():
        def done(i, carry):
            anchor_copy(n - i).wait_send()
            return carry

        lax.fori_loop(1, n, done, 0)

    @pl.when(h > 0)
    def _():
        def done(j, carry):
            kept_copy(h, j).wait_send()
            return carry

        lax.fori_loop(h + 1, n, done, 0)


def shards(n, tps, queries, key_rows, value_rows, retained):
    rows, width = queries.shape
    hd = key_rows.shape[1]
    keep = retained.shape[2]
    steps = width // hd // heads_per_step
    far = rows + -(-(n - 2) * keep // hd) * hd
    any_spec = pl.BlockSpec(memory_space=pl.ANY)
    return pl.pallas_call(
        functools.partial(kernel, n, tps, far),
        out_shape=jax.ShapeDtypeStruct((rows // tps, width * tps), queries.dtype),
        in_specs=[any_spec] * 4,
        out_specs=any_spec,
        scratch_shapes=[
            pltpu.VMEM((rows, width), jnp.bfloat16),
            pltpu.VMEM((far + rows, 3 * hd), jnp.bfloat16),
            pltpu.VMEM((keep, 2 * hd), jnp.bfloat16),
            pltpu.VMEM((1, 1, keep), jnp.int32),
            pltpu.VMEM((width // hd * rows, rows), jnp.float32),
            pltpu.VMEM((rows, width), jnp.bfloat16),
            pltpu.SemaphoreType.DMA((4,)),
            pltpu.SemaphoreType.DMA((n,)),
            pltpu.SemaphoreType.DMA((n,)),
            pltpu.SemaphoreType.DMA((tps, steps)),
            pltpu.SemaphoreType.DMA((tps, steps)),
            pltpu.SemaphoreType.DMA((steps,)),
        ],
        compiler_params=pltpu.CompilerParams(
            collective_id=0, has_side_effects=True, vmem_limit_bytes=48 * 1024 * 1024
        ),
        cost_estimate=pl.CostEstimate(
            flops=4 * width * rows * (far + rows),
            bytes_accessed=4 * rows * width,
            transcendentals=width // hd * rows * (far + rows),
        ),
    )(queries, key_rows, value_rows, retained)


def solution(mesh):
    in_specs = (P("ctx", "tp"), P("ctx", "tp"), P("ctx", "tp"), P("ctx", "tp", None))
    out_specs = P(("ctx", "tp"), None)
    return jax.shard_map(
        functools.partial(shards, mesh.shape["ctx"], mesh.shape["tp"]),
        mesh=mesh, in_specs=in_specs, out_specs=out_specs, check_vma=False,
    )
```

time: 118 us -> 25.8 us (0.22)
  waiting for transfers between devices: 51.8 us -> 0 us
  blocking collectives: 44.3 us -> 0 us
  Pallas kernels: 0 us -> 21.7 us
  between operations: 13.5 us -> 0.01 us
  matrix products: 2.55 us -> 0 us
  other arithmetic: 1.91 us -> 0 us
    psum x1 -> x0, waiting for transfers between devices: 51.8 us -> none  [from_root(): return lax.psum(block, axis)]
    all_gather x2 -> x0, blocking collectives: 36.6 us -> none  [the longest x1 19 us: shards(): piece_keys = lax.all_gather(kept_keys, 'ctx', axis=0, tiled=True)]
    pallas_call x0 -> x1, Pallas kernels: none -> 21.7 us  [shards(): pl.pallas_call(functools.partial(kernel, n, tps, far), out_shape=jax.Shap...]
    all_to_all x1 -> x0, blocking collectives: 7.71 us -> none  [shards(): return lax.all_to_all(result, 'tp', split_axis=0, concat_axis=1, tiled=True)]
    dot_general x6 -> x0, matrix products: 2.55 us -> none  [the longest x2 1.3 us: fold_block(): jnp.einsum('bjd,kd->bjk', query_heads, key_block, preferred_element_type=...]
    unnamed x10 -> x9, local copies, waits for them, and re-layouts: 1.32 us -> 3.82 us
    select_n x3 -> x0, other arithmetic: 1.53 us -> none  [the longest x1 1.46 us: from_root(): jnp.where(lax.axis_index(axis) == holder, block, jnp.zeros_like(block))]
  transfers between devices with their start and end apart: 1 -> 0, of which waited for: 1 -> 0; matrix products, arithmetic and copies ran while one was open for 2% -> 0% of each run, Pallas kernels for 0% -> 0%
where the time goes in v1:
time: 25.8 us; the launch traced here: 25.5 us
  Pallas kernels  21.7 us (84%)
  local copies, waits for them, and re-layouts  3.82 us (15%)
    pallas_call x1, Pallas kernels, shards(): pl.pallas_call(functools.partial(kernel, n, tps, far), out_shape=jax.Shap...  21.7 us
    unnamed x9, local copies, waits for them, and re-layouts  3.82 us

profile of v1, /device:TPU:8, one launch (start us, length us, event | category | flops | bytes accessed | tf_op | source)
XLA Modules:
  0.0 25.5 jit_solution(4720807343651605124)
XLA Ops:
  0.0 0.0 copy-start
  0.0 0.9 %copy-done = bf16[128,1024]{1,0:T(8,128)(2,1)S(1)} copy-done((bf16[128,1024]{1,0:T(8,128)(2,1)S(1)}, bf16[128,1024]{1,0:T(8,128)(2,1)}, u32[]{:S(2)}) %copy-start) | copy-done | bytes 262168
  1.0 0.0 copy-start.1
  1.0 0.8 %copy-done.1 = bf16[128,128]{1,0:T(8,128)(2,1)S(1)} copy-done((bf16[128,128]{1,0:T(8,128)(2,1)S(1)}, bf16[128,128]{1,0:T(8,128)(2,1)}, u32[]{:S(2)}) %copy-start.1) | copy-done | bytes 32792
  1.7 0.0 copy-start.2
  1.7 0.8 %copy-done.2 = bf16[128,128]{1,0:T(8,128)(2,1)S(1)} copy-done((bf16[128,128]{1,0:T(8,128)(2,1)S(1)}, bf16[128,128]{1,0:T(8,128)(2,1)}, u32[]{:S(2)}) %copy-start.2) | copy-done | bytes 32792
  2.5 0.0 copy-start.3
  2.5 0.7 %copy-done.3 = s32[1,1,16]{2,1,0:T(1,128)S(1)} copy-done((s32[1,1,16]{2,1,0:T(1,128)S(1)}, s32[1,1,16]{2,1,0:T(1,128)}, u32[]{:S(2)}) %copy-start.3) | copy-done | bytes 88
  3.1 21.7 %shard_map.46 = bf16[64,2048]{1,0:T(8,128)(2,1)S(1)} custom-call(bf16[128,1024]{1,0:T(8,128)(2,1)S(1)} %copy-done, bf16[128,128]{1,0:T(8,128)(2,1)S(1)} %copy-done.1, bf16[128,128]{1,0:T(8,128)(2,1)S(1)} %copy-done.2, s32[1,1,16]{2,1,0:T(1,128)S(1)} %copy-done.3), custom_call_target="tpu_custom_call" | custom-call | flops 268435456 | bytes 524288 | tf_op jit(solution)/shard_map/pallas_call | solution.py:218
  24.8 0.7 %copy.6 = bf16[64,2048]{1,0:T(8,128)(2,1)} copy(bf16[64,2048]{1,0:T(8,128)(2,1)S(1)} %shard_map.46) | data formatting | bytes 524288
Async XLA Ops:
  0.0 0.9 %copy-start = (bf16[128,1024]{1,0:T(8,128)(2,1)S(1)}, bf16[128,1024]{1,0:T(8,128)(2,1)}, u32[]{:S(2)}) copy-start(bf16[128,1024]{1,0:T(8,128)(2,1)} %q_hbm.1) | copy-start | bytes 786436
  1.0 0.8 %copy-start.1 = (bf16[128,128]{1,0:T(8,128)(2,1)S(1)}, bf16[128,128]{1,0:T(8,128)(2,1)}, u32[]{:S(2)}) copy-start(bf16[128,128]{1,0:T(8,128)(2,1)} %k_hbm.1) | copy-start | bytes 98308
  1.7 0.8 %copy-start.2 = (bf16[128,128]{1,0:T(8,128)(2,1)S(1)}, bf16[128,128]{1,0:T(8,128)(2,1)}, u32[]{:S(2)}) copy-start(bf16[128,128]{1,0:T(8,128)(2,1)} %v_hbm.1) | copy-start | bytes 98308
  2.5 0.7 %copy-start.3 = (s32[1,1,16]{2,1,0:T(1,128)S(1)}, s32[1,1,16]{2,1,0:T(1,128)}, u32[]{:S(2)}) copy-start(s32[1,1,16]{2,1,0:T(1,128)} %pick_hbm.1) | copy-start | bytes 196

commit v2 on v1

v2 whole, which is shorter than its diff:
```python
import functools
import math

import jax
import jax.numpy as jnp
from jax import lax
from jax.experimental import pallas as pl
from jax.experimental.pallas import tpu as pltpu
from jax.sharding import PartitionSpec as P

MESH = pl.DeviceIdType.MESH
piece_rows = 16
turn_rows = 32


def kernel(
    n, tps, far, turn, q_hbm, k_hbm, v_hbm, pick_hbm, out,
    q, kv, kept, picks, local_scores, stage,
    load_sem, kv_send, kept_recv, piece_send, piece_recv, out_send, out_recv, own_sem,
):
    rows, width = q_hbm.shape
    hd = k_hbm.shape[1]
    keep = picks.shape[2]
    group = width // hd
    part = rows // tps
    subs = part // turn
    pieces = rows // piece_rows
    first_relay = n - pieces
    h = lax.axis_index("ctx")
    t = lax.axis_index("tp")
    scale = math.log2(math.e) / math.sqrt(hd)

    loads = [
        pltpu.make_async_copy(k_hbm, kv.at[pl.ds(far, rows), pl.ds(0, hd)], load_sem.at[0]),
        pltpu.make_async_copy(v_hbm, kv.at[pl.ds(far, rows), pl.ds(hd, hd)], load_sem.at[1]),
        pltpu.make_async_copy(pick_hbm, picks, load_sem.at[2]),
        pltpu.make_async_copy(q_hbm, q, load_sem.at[3]),
    ]
    for load in loads:
        load.start()
    kv[0:far, 0 : 2 * hd] = jnp.zeros((far, 2 * hd), kv.dtype)
    kv[:, 2 * hd :] = jnp.ones((far + rows, hd), kv.dtype)

    barrier = pltpu.get_barrier_semaphore()

    def greet(j, carry):
        pl.semaphore_signal(barrier, inc=1, device_id={"ctx": j}, device_id_type=MESH)
        return carry

    relay = h >= first_relay

    @pl.when(h > 0)
    def _():
        lax.fori_loop(jnp.where(relay, 0, 1), h, greet, 0)
        lax.fori_loop(jnp.maximum(h + 1, first_relay), n, greet, 0)

    for d in range(1, tps):
        pl.semaphore_signal(
            barrier, inc=1, device_id={"tp": lax.rem(t + d, tps)}, device_id_type=MESH
        )

    def scatter_copy(p):
        return pltpu.make_async_remote_copy(
            src_ref=kv.at[pl.ds(far + p * piece_rows, piece_rows), pl.ds(0, 2 * hd)],
            dst_ref=kv.at[pl.ds(p * piece_rows, piece_rows), pl.ds(0, 2 * hd)],
            send_sem=piece_send.at[p],
            recv_sem=piece_recv.at[p],
            device_id={"ctx": first_relay + p},
            device_id_type=MESH,
        )

    def piece_copy(p, j):
        return pltpu.make_async_remote_copy(
            src_ref=kv.at[pl.ds(p * piece_rows, piece_rows), pl.ds(0, 2 * hd)],
            dst_ref=kv.at[pl.ds(p * piece_rows, piece_rows), pl.ds(0, 2 * hd)],
            send_sem=piece_send.at[j],
            recv_sem=piece_recv.at[p],
            device_id={"ctx": j},
            device_id_type=MESH,
        )

    def kept_copy(owner, j):
        return pltpu.make_async_remote_copy(
            src_ref=kept,
            dst_ref=kv.at[pl.ds(rows + keep * (owner - 1), keep), pl.ds(0, 2 * hd)],
            send_sem=kv_send.at[j],
            recv_sem=kept_recv.at[owner],
            device_id={"ctx": j},
            device_id_type=MESH,
        )

    def loop(low, high, act):
        def body(j, carry):
            act(j)
            return carry

        lax.fori_loop(low, high, body, 0)

    loads[0].wait()
    loads[1].wait()
    reached = jnp.where(h == 0, pieces, jnp.where(relay, n - 2, n - 1 - h))
    pl.semaphore_wait(barrier, reached + (tps - 1))

    @pl.when(h == 0)
    def _():
        loop(0, pieces, lambda p: scatter_copy(p).start())

    loads[2].wait()
    hit = lax.broadcasted_iota(jnp.int32, (rows, keep), 0) == picks[0]
    kept[...] = lax.dot_general(
        hit.astype(jnp.float32).astype(jnp.bfloat16),
        kv[far:, 0 : 2 * hd],
        (((0,), (0,)), ((), ())),
        preferred_element_type=jnp.float32,
    ).astype(kept.dtype)

    @pl.when(h > 0)
    def _():
        loop(h + 1, n, lambda j: kept_copy(h, j).start())

    @pl.when(relay)
    def _():
        p = h - first_relay
        piece_copy(p, 0).wait_recv()
        loop(h + 1, n, lambda j: piece_copy(p, j).start())
        loop(1, h, lambda j: piece_copy(p, j).start())

    loads[3].wait()
    tall = group * turn
    contract = (((1,), (1,)), ((), ()))
    row_of = jnp.concatenate([lax.broadcasted_iota(jnp.int32, (turn, rows), 0)] * group, axis=0)
    column = lax.broadcasted_iota(jnp.int32, (tall, rows), 1)

    order = [(d % tps, sub) for d in range(1, tps + 1) for sub in range(subs)]

    def begin(step):
        d, sub = order[step]
        return pl.multiple_of(lax.rem(t + d, tps) * part + sub * turn, turn)

    def head_rows(step):
        return jnp.concatenate(
            [q[pl.ds(begin(step), turn), i * hd : (i + 1) * hd] for i in range(group)], axis=0
        )

    for step in range(len(order)):
        local_scores[step * tall : (step + 1) * tall, :] = jnp.where(
            column <= row_of + begin(step),
            lax.dot_general(
                head_rows(step), kv[far:, 0:hd], contract, preferred_element_type=jnp.float32
            ),
            -jnp.inf,
        )

    @pl.when(h > 0)
    def _():
        loop(1, h, lambda j: kept_copy(j, 0).wait_recv())

        def arrive(p):
            @pl.when(h != first_relay + p)
            def _():
                piece_copy(p, 0).wait_recv()

        loop(0, pieces, arrive)

    limit = jnp.where(h > 0, rows + keep * (h - 1), 0)
    bias = jnp.where(lax.broadcasted_iota(jnp.int32, (1, far), 1) < limit, 0.0, -jnp.inf)

    def out_copy(step, target, source):
        sub = order[step][1]
        return pltpu.make_async_remote_copy(
            src_ref=stage.at[pl.ds(begin(step), turn), :],
            dst_ref=out.at[pl.ds(sub * turn, turn), pl.ds(pl.multiple_of(source * width, width), width)],
            send_sem=out_send.at[step],
            recv_sem=out_recv.at[source, sub],
            device_id={"tp": target},
            device_id_type=MESH,
        )

    def own_copy(step):
        sub = order[step][1]
        return pltpu.make_async_copy(
            stage.at[pl.ds(begin(step), turn), :],
            out.at[pl.ds(sub * turn, turn), pl.ds(pl.multiple_of(t * width, width), width)],
            own_sem.at[sub],
        )

    for step in range(len(order)):
        scores = (
            lax.dot_general(
                head_rows(step), kv[0:far, 0:hd], contract, preferred_element_type=jnp.float32
            )
            + bias
        )
        own = local_scores[step * tall : (step + 1) * tall, :]
        top = jnp.maximum(
            jnp.max(scores, axis=1, keepdims=True), jnp.max(own, axis=1, keepdims=True)
        )
        weights = jnp.concatenate(
            [
                jnp.exp2((scores - top) * scale).astype(jnp.bfloat16),
                jnp.exp2((own - top) * scale).astype(jnp.bfloat16),
            ],
            axis=1,
        )
        summed = jnp.dot(weights, kv[:, hd:], preferred_element_type=jnp.float32)
        result = (summed[:, 0:hd] / summed[:, hd:]).astype(stage.dtype)
        for i in range(group):
            stage[pl.ds(begin(step), turn), i * hd : (i + 1) * hd] = result[
                i * turn : (i + 1) * turn
            ]
        d = order[step][0]
        if d:
            out_copy(step, lax.rem(t + d, tps), t).start()
        else:
            own_copy(step).start()

    @pl.when(h == 0)
    def _():
        loop(0, pieces, lambda p: scatter_copy(p).wait_send())

    @pl.when(h > 0)
    def _():
        loop(h + 1, n, lambda j: kept_copy(h, j).wait_send())

    @pl.when(relay)
    def _():
        p = h - first_relay
        loop(h + 1, n, lambda j: piece_copy(p, j).wait_send())
        loop(1, h, lambda j: piece_copy(p, j).wait_send())

    for step in range(len(order)):
        d = order[step][0]
        if d:
            other = lax.rem(t + d, tps)
            out_copy(step, other, t).wait_send()
            out_copy(step, other, other).wait_recv()
        else:
            own_copy(step).wait()


def shards(n, tps, queries, key_rows, value_rows, retained):
    rows, width = queries.shape
    hd = key_rows.shape[1]
    keep = retained.shape[2]
    part = rows // tps
    turn = min(turn_rows, part)
    subs = part // turn
    far = rows + -(-(n - 2) * keep // hd) * hd
    any_spec = pl.BlockSpec(memory_space=pl.ANY)
    return pl.pallas_call(
        functools.partial(kernel, n, tps, far, turn),
        out_shape=jax.ShapeDtypeStruct((rows // tps, width * tps), queries.dtype),
        in_specs=[any_spec] * 4,
        out_specs=any_spec,
        scratch_shapes=[
            pltpu.VMEM((rows, width), jnp.bfloat16),
            pltpu.VMEM((far + rows, 3 * hd), jnp.bfloat16),
            pltpu.VMEM((keep, 2 * hd), jnp.bfloat16),
            pltpu.VMEM((1, 1, keep), jnp.int32),
            pltpu.VMEM((width // hd * rows, rows), jnp.float32),
            pltpu.VMEM((rows, width), jnp.bfloat16),
            pltpu.SemaphoreType.DMA((4,)),
            pltpu.SemaphoreType.DMA((n,)),
            pltpu.SemaphoreType.DMA((n,)),
            pltpu.SemaphoreType.DMA((n,)),
            pltpu.SemaphoreType.DMA((rows // piece_rows,)),
            pltpu.SemaphoreType.DMA((tps * subs,)),
            pltpu.SemaphoreType.DMA((tps, subs)),
            pltpu.SemaphoreType.DMA((subs,)),
        ],
        compiler_params=pltpu.CompilerParams(
            collective_id=0, has_side_effects=True, vmem_limit_bytes=63 * 1024 * 1024
        ),
        cost_estimate=pl.CostEstimate(
            flops=4 * width * rows * (far + rows),
            bytes_accessed=4 * rows * width,
            transcendentals=width // hd * rows * (far + rows),
        ),
    )(queries, key_rows, value_rows, retained)


def solution(mesh):
    in_specs = (P("ctx", "tp"), P("ctx", "tp"), P("ctx", "tp"), P("ctx", "tp", None))
    out_specs = P(("ctx", "tp"), None)
    return jax.shard_map(
        functools.partial(shards, mesh.shape["ctx"], mesh.shape["tp"]),
        mesh=mesh, in_specs=in_specs, out_specs=out_specs, check_vma=False,
    )
```

time: 25.8 us -> 21.6 us (0.84)
  local copies, waits for them, and re-layouts: 3.82 us -> 1.67 us
  Pallas kernels: 21.7 us -> 19.7 us
    unnamed x9 -> x1, local copies, waits for them, and re-layouts: 3.82 us -> 1.67 us
    pallas_call x1, Pallas kernels: 21.7 us -> 19.7 us  [shards(): pl.pallas_call(functools.partial(kernel, n, tps, far, turn), out_shape=ja...]
where the time goes in v2:
time: 21.6 us; the launch traced here: 21.4 us
  Pallas kernels  19.7 us (91%)
  local copies, waits for them, and re-layouts  1.67 us (8%)
    pallas_call x1, Pallas kernels, shards(): pl.pallas_call(functools.partial(kernel, n, tps, far, turn), out_shape=ja...  19.7 us
    unnamed x1, local copies, waits for them, and re-layouts  1.67 us

profile of v2, /device:TPU:8, one launch (start us, length us, event | category | flops | bytes accessed | tf_op | source)
XLA Modules:
  0.0 21.4 jit_solution(2257731086523884279)
XLA Ops:
  0.0 19.7 %shard_map.46 = bf16[64,2048]{1,0:T(8,128)(2,1)} custom-call(bf16[128,1024]{1,0:T(8,128)(2,1)} %q_hbm.1, bf16[128,128]{1,0:T(8,128)(2,1)} %k_hbm.1, bf16[128,128]{1,0:T(8,128)(2,1)} %v_hbm.1, s32[1,1,16]{2,1,0:T(1,128)} %pick_hbm.1), custom_call_target="tpu_custom_call" | custom-call | flops 268435456 | bytes 524288 | tf_op jit(solution)/shard_map/pallas_call | solution.py:250
  19.7 1.7 %copy.6 = bf16[64,2048]{1,0:T(8,128)(2,1)} copy(bf16[64,2048]{1,0:T(8,128)(2,1)} %shard_map.46) | data formatting | bytes 524288

commit v3 on v2

--- a/solution.py
+++ b/solution.py
@@ -9,14 +9,13 @@
 from jax.sharding import PartitionSpec as P
 
 MESH = pl.DeviceIdType.MESH
-piece_rows = 16
 turn_rows = 32
 
 
 def kernel(
     n, tps, far, turn, q_hbm, k_hbm, v_hbm, pick_hbm, out,
     q, kv, kept, picks, local_scores, stage,
-    load_sem, kv_send, kept_recv, piece_send, piece_recv, out_send, out_recv, own_sem,
+    load_sem, ready, kept_send, kept_recv, half_send, half_recv, out_send, out_recv, own_sem,
 ):
     rows, width = q_hbm.shape
     hd = k_hbm.shape[1]
@@ -24,8 +23,7 @@
     group = width // hd
     part = rows // tps
     subs = part // turn
-    pieces = rows // piece_rows
-    first_relay = n - pieces
+    half = rows // 2
     h = lax.axis_index("ctx")
     t = lax.axis_index("tp")
     scale = math.log2(math.e) / math.sqrt(hd)
@@ -43,39 +41,39 @@
 
     barrier = pltpu.get_barrier_semaphore()
 
-    def greet(j, carry):
+    def loop(low, high, act):
+        def body(j, carry):
+            act(j)
+            return carry
+
+        lax.fori_loop(low, high, body, 0)
+
+    def greet(j):
         pl.semaphore_signal(barrier, inc=1, device_id={"ctx": j}, device_id_type=MESH)
-        return carry
-
-    relay = h >= first_relay
-
-    @pl.when(h > 0)
-    def _():
-        lax.fori_loop(jnp.where(relay, 0, 1), h, greet, 0)
-        lax.fori_loop(jnp.maximum(h + 1, first_relay), n, greet, 0)
 
     for d in range(1, tps):
         pl.semaphore_signal(
             barrier, inc=1, device_id={"tp": lax.rem(t + d, tps)}, device_id_type=MESH
         )
-
-    def scatter_copy(p):
+    loop(h + 1, n, greet)
+
+    def half_copy(side, base, j):
         return pltpu.make_async_remote_copy(
-            src_ref=kv.at[pl.ds(far + p * piece_rows, piece_rows), pl.ds(0, 2 * hd)],
-            dst_ref=kv.at[pl.ds(p * piece_rows, piece_rows), pl.ds(0, 2 * hd)],
-            send_sem=piece_send.at[p],
-            recv_sem=piece_recv.at[p],
-            device_id={"ctx": first_relay + p},
+            src_ref=kv.at[pl.ds(base + side * half, half), pl.ds(0, 2 * hd)],
+            dst_ref=kv.at[pl.ds(side * half, half), pl.ds(0, 2 * hd)],
+            send_sem=half_send.at[j],
+            recv_sem=half_recv.at[side],
+            device_id={"ctx": j},
             device_id_type=MESH,
         )
 
-    def piece_copy(p, j):
+    def second_half():
         return pltpu.make_async_remote_copy(
-            src_ref=kv.at[pl.ds(p * piece_rows, piece_rows), pl.ds(0, 2 * hd)],
-            dst_ref=kv.at[pl.ds(p * piece_rows, piece_rows), pl.ds(0, 2 * hd)],
-            send_sem=piece_send.at[j],
-            recv_sem=piece_recv.at[p],
-            device_id={"ctx": j},
+            src_ref=kv.at[pl.ds(far + half, half), pl.ds(0, 2 * hd)],
+            dst_ref=kv.at[pl.ds(half, half), pl.ds(0, 2 * hd)],
+            send_sem=half_send.at[0],
+            recv_sem=half_recv.at[1],
+            device_id={"ctx": 1},
             device_id_type=MESH,
         )
 
@@ -83,28 +81,14 @@
         return pltpu.make_async_remote_copy(
             src_ref=kept,
             dst_ref=kv.at[pl.ds(rows + keep * (owner - 1), keep), pl.ds(0, 2 * hd)],
-            send_sem=kv_send.at[j],
+            send_sem=kept_send.at[j],
             recv_sem=kept_recv.at[owner],
             device_id={"ctx": j},
             device_id_type=MESH,
         )
 
-    def loop(low, high, act):
-        def body(j, carry):
-            act(j)
-            return carry
-
-        lax.fori_loop(low, high, body, 0)
-
     loads[0].wait()
     loads[1].wait()
-    reached = jnp.where(h == 0, pieces, jnp.where(relay, n - 2, n - 1 - h))
-    pl.semaphore_wait(barrier, reached + (tps - 1))
-
-    @pl.when(h == 0)
-    def _():
-        loop(0, pieces, lambda p: scatter_copy(p).start())
-
     loads[2].wait()
     hit = lax.broadcasted_iota(jnp.int32, (rows, keep), 0) == picks[0]
     kept[...] = lax.dot_general(
@@ -114,16 +98,61 @@
         preferred_element_type=jnp.float32,
     ).astype(kept.dtype)
 
-    @pl.when(h > 0)
-    def _():
-        loop(h + 1, n, lambda j: kept_copy(h, j).start())
-
-    @pl.when(relay)
-    def _():
-        p = h - first_relay
-        piece_copy(p, 0).wait_recv()
-        loop(h + 1, n, lambda j: piece_copy(p, j).start())
-        loop(1, h, lambda j: piece_copy(p, j).start())
+    pl.semaphore_wait(barrier, h + (tps - 1))
+
+    def tell(j):
+        pl.semaphore_signal(ready.at[h], inc=1, device_id={"ctx": j}, device_id_type=MESH)
+
+    loop(0, h, tell)
+
+    @pl.when(h == 0)
+    def _():
+        def serve(j):
+            pl.semaphore_wait(ready.at[j], 1)
+
+            @pl.when(j == 1)
+            def _():
+                second_half().start()
+
+            @pl.when((j == 1) | (lax.rem(j, 2) == 0))
+            def _():
+                half_copy(0, far, j).start()
+
+        loop(1, n, serve)
+
+    @pl.when(h == 1)
+    def _():
+        half_copy(1, 0, 0).wait_recv()
+
+        def serve(j):
+            pl.semaphore_wait(ready.at[j], 1)
+
+            @pl.when(lax.rem(j, 2) == 1)
+            def _():
+                half_copy(1, 0, j).start()
+
+            kept_copy(1, j).start()
+
+        loop(2, n, serve)
+        half_copy(0, 0, 0).wait_recv()
+
+    @pl.when(h > 1)
+    def _():
+        def serve(j):
+            pl.semaphore_wait(ready.at[j], 1)
+            kept_copy(h, j).start()
+
+        loop(h + 1, n, serve)
+
+        @pl.when(lax.rem(h, 2) == 0)
+        def _():
+            half_copy(0, 0, 0).wait_recv()
+            half_copy(0, 0, h + 1).start()
+
+        @pl.when(lax.rem(h, 2) == 1)
+        def _():
+            half_copy(1, 0, 0).wait_recv()
+            half_copy(1, 0, h - 1).start()
 
     loads[3].wait()
     tall = group * turn
@@ -151,16 +180,17 @@
             -jnp.inf,
         )
 
-    @pl.when(h > 0)
-    def _():
-        loop(1, h, lambda j: kept_copy(j, 0).wait_recv())
-
-        def arrive(p):
-            @pl.when(h != first_relay + p)
-            def _():
-                piece_copy(p, 0).wait_recv()
-
-        loop(0, pieces, arrive)
+    loop(1, h, lambda j: kept_copy(j, 0).wait_recv())
+
+    @pl.when(h > 1)
+    def _():
+        @pl.when(lax.rem(h, 2) == 0)
+        def _():
+            half_copy(1, 0, 0).wait_recv()
+
+        @pl.when(lax.rem(h, 2) == 1)
+        def _():
+            half_copy(0, 0, 0).wait_recv()
 
     limit = jnp.where(h > 0, rows + keep * (h - 1), 0)
     bias = jnp.where(lax.broadcasted_iota(jnp.int32, (1, far), 1) < limit, 0.0, -jnp.inf)
@@ -216,17 +246,25 @@
 
     @pl.when(h == 0)
     def _():
-        loop(0, pieces, lambda p: scatter_copy(p).wait_send())
+        second_half().wait_send()
+        half_copy(0, far, 1).wait_send()
+        loop(1, n // 2, lambda i: half_copy(0, far, 2 * i).wait_send())
+
+    @pl.when(h == 1)
+    def _():
+        loop(1, n // 2, lambda i: half_copy(1, 0, 2 * i + 1).wait_send())
 
     @pl.when(h > 0)
     def _():
         loop(h + 1, n, lambda j: kept_copy(h, j).wait_send())
 
-    @pl.when(relay)
-    def _():
-        p = h - first_relay
-        loop(h + 1, n, lambda j: piece_copy(p, j).wait_send())
-        loop(1, h, lambda j: piece_copy(p, j).wait_send())
+    @pl.when((h > 1) & (lax.rem(h, 2) == 0))
+    def _():
+        half_copy(0, 0, h + 1).wait_send()
+
+    @pl.when((h > 1) & (lax.rem(h, 2) == 1))
+    def _():
+        half_copy(1, 0, h - 1).wait_send()
 
     for step in range(len(order)):
         d = order[step][0]
@@ -260,23 +298,24 @@
             pltpu.VMEM((width // hd * rows, rows), jnp.float32),
             pltpu.VMEM((rows, width), jnp.bfloat16),
             pltpu.SemaphoreType.DMA((4,)),
+            pltpu.SemaphoreType.REGULAR((n,)),
             pltpu.SemaphoreType.DMA((n,)),
             pltpu.SemaphoreType.DMA((n,)),
             pltpu.SemaphoreType.DMA((n,)),
-            pltpu.SemaphoreType.DMA((rows // piece_rows,)),
+            pltpu.SemaphoreType.DMA((2,)),
             pltpu.SemaphoreType.DMA((tps * subs,)),
             pltpu.SemaphoreType.DMA((tps, subs)),
             pltpu.SemaphoreType.DMA((subs,)),
         ],
         compiler_params=pltpu.CompilerParams(
-            collective_id=0, has_side_effects=True, vmem_limit_bytes=63 * 1024 * 1024
+            collective_id=0, has_side_effects=True, vmem_limit_bytes=48 * 1024 * 1024
         ),
         cost_estimate=pl.CostEstimate(
             flops=4 * width * rows * (far + rows),
             bytes_accessed=4 * rows * width,
             transcendentals=width // hd * rows * (far + rows),
         ),
-    )(queries, key_rows, value_rows, retained)
+    )(*(pltpu.with_memory_space_constraint(x, pltpu.HBM) for x in (queries, key_rows, value_rows, retained)))
 
 
 def solution(mesh):

time: 21.6 us -> 17.4 us (0.81)
  the two profiles are of different devices: /device:TPU:8 before, /device:TPU:28 now
where the time goes in v3:
time: 17.4 us; the launch traced here: 17.3 us
  Pallas kernels  16.6 us (95%)
  local copies, waits for them, and re-layouts  0.71 us (4%)
    pallas_call x1, Pallas kernels, shards(): pl.pallas_call(functools.partial(kernel, n, tps, far, turn), out_shape=ja...  16.6 us
    unnamed x1, local copies, waits for them, and re-layouts  0.71 us

profile of v3, /device:TPU:28, one launch (start us, length us, event | category | flops | bytes accessed | tf_op | source)
XLA Modules:
  0.0 17.3 jit_solution(11864399133515574249)
XLA Ops:
  0.0 16.6 %shard_map.46 = bf16[64,2048]{1,0:T(8,128)(2,1)S(1)} custom-call(bf16[128,1024]{1,0:T(8,128)(2,1)} %q_hbm.1, bf16[128,128]{1,0:T(8,128)(2,1)} %k_hbm.1, bf16[128,128]{1,0:T(8,128)(2,1)} %v_hbm.1, s32[1,1,16]{2,1,0:T(1,128)} %pick_hbm.1), custom_call_target="tpu_custom_call" | custom-call | flops 268435456 | bytes 524288 | tf_op jit(solution)/shard_map/pallas_call | solution.py:288
  16.6 0.7 %copy.6 = bf16[64,2048]{1,0:T(8,128)(2,1)} copy(bf16[64,2048]{1,0:T(8,128)(2,1)S(1)} %shard_map.46) | data formatting | bytes 524288

commit v4 on v3

--- a/solution.py
+++ b/solution.py
@@ -15,7 +15,7 @@
 def kernel(
     n, tps, far, turn, q_hbm, k_hbm, v_hbm, pick_hbm, out,
     q, kv, kept, picks, local_scores, stage,
-    load_sem, ready, kept_send, kept_recv, half_send, half_recv, out_send, out_recv, own_sem,
+    load_sem, ready, forward_send, kept_send, kept_recv, half_send, half_recv, out_send, out_recv, own_sem,
 ):
     rows, width = q_hbm.shape
     hd = k_hbm.shape[1]
@@ -24,8 +24,11 @@
     part = rows // tps
     subs = part // turn
     half = rows // 2
+    chips = n // 2
     h = lax.axis_index("ctx")
     t = lax.axis_index("tp")
+    c, p = h // 2, lax.rem(h, 2)
+    mate = h + 1 - 2 * p
     scale = math.log2(math.e) / math.sqrt(hd)
 
     loads = [
@@ -55,7 +58,8 @@
         pl.semaphore_signal(
             barrier, inc=1, device_id={"tp": lax.rem(t + d, tps)}, device_id_type=MESH
         )
-    loop(h + 1, n, greet)
+    greet(mate)
+    loop(c + 1, chips, lambda i: greet(2 * i + p))
 
     def half_copy(side, base, j):
         return pltpu.make_async_remote_copy(
@@ -84,6 +88,17 @@
             send_sem=kept_send.at[j],
             recv_sem=kept_recv.at[owner],
             device_id={"ctx": j},
+            device_id_type=MESH,
+        )
+
+    def forward_copy(owner):
+        slot = kv.at[pl.ds(rows + keep * (owner - 1), keep), pl.ds(0, 2 * hd)]
+        return pltpu.make_async_remote_copy(
+            src_ref=slot,
+            dst_ref=slot,
+            send_sem=forward_send.at[owner],
+            recv_sem=kept_recv.at[owner],
+            device_id={"ctx": mate},
             device_id_type=MESH,
         )
 
@@ -98,61 +113,57 @@
         preferred_element_type=jnp.float32,
     ).astype(kept.dtype)
 
-    pl.semaphore_wait(barrier, h + (tps - 1))
-
-    def tell(j):
-        pl.semaphore_signal(ready.at[h], inc=1, device_id={"ctx": j}, device_id_type=MESH)
-
-    loop(0, h, tell)
+    pl.semaphore_wait(barrier, c + tps)
+
+    def tell(i):
+        pl.semaphore_signal(ready.at[h], inc=1, device_id={"ctx": 2 * i + p}, device_id_type=MESH)
+
+    loop(0, c, tell)
 
     @pl.when(h == 0)
     def _():
-        def serve(j):
-            pl.semaphore_wait(ready.at[j], 1)
-
-            @pl.when(j == 1)
-            def _():
-                second_half().start()
-
-            @pl.when((j == 1) | (lax.rem(j, 2) == 0))
-            def _():
-                half_copy(0, far, j).start()
-
-        loop(1, n, serve)
+        second_half().start()
+
+        def serve(i):
+            pl.semaphore_wait(ready.at[2 * i], 1)
+            half_copy(0, far, 2 * i).start()
+
+        loop(1, 2, serve)
+        half_copy(0, far, 1).start()
+        loop(2, chips, serve)
 
     @pl.when(h == 1)
     def _():
         half_copy(1, 0, 0).wait_recv()
 
-        def serve(j):
-            pl.semaphore_wait(ready.at[j], 1)
-
-            @pl.when(lax.rem(j, 2) == 1)
-            def _():
-                half_copy(1, 0, j).start()
-
-            kept_copy(1, j).start()
-
-        loop(2, n, serve)
+        def serve(i):
+            pl.semaphore_wait(ready.at[2 * i + 1], 1)
+            half_copy(1, 0, 2 * i + 1).start()
+            kept_copy(1, 2 * i + 1).start()
+
+        loop(1, chips, serve)
         half_copy(0, 0, 0).wait_recv()
 
-    @pl.when(h > 1)
-    def _():
-        def serve(j):
-            pl.semaphore_wait(ready.at[j], 1)
-            kept_copy(h, j).start()
-
-        loop(h + 1, n, serve)
-
-        @pl.when(lax.rem(h, 2) == 0)
+    @pl.when(c > 0)
+    def _():
+        @pl.when(p == 0)
         def _():
-            half_copy(0, 0, 0).wait_recv()
-            half_copy(0, 0, h + 1).start()
-
-        @pl.when(lax.rem(h, 2) == 1)
-        def _():
-            half_copy(1, 0, 0).wait_recv()
-            half_copy(1, 0, h - 1).start()
+            kept_copy(h, h + 1).start()
+
+        def serve(i):
+            pl.semaphore_wait(ready.at[2 * i + p], 1)
+            kept_copy(h, 2 * i + p).start()
+
+        loop(c + 1, chips, serve)
+        half_copy(p, 0, 0).wait_recv()
+        half_copy(p, 0, mate).start()
+
+        def forward(i):
+            owner = 2 * i + p
+            forward_copy(owner).wait_recv()
+            forward_copy(owner).start()
+
+        loop(1 - p, c, forward)
 
     loads[3].wait()
     tall = group * turn
@@ -180,17 +191,10 @@
             -jnp.inf,
         )
 
-    loop(1, h, lambda j: kept_copy(j, 0).wait_recv())
-
-    @pl.when(h > 1)
-    def _():
-        @pl.when(lax.rem(h, 2) == 0)
-        def _():
-            half_copy(1, 0, 0).wait_recv()
-
-        @pl.when(lax.rem(h, 2) == 1)
-        def _():
-            half_copy(0, 0, 0).wait_recv()
+    @pl.when(c > 0)
+    def _():
+        half_copy(1 - p, 0, 0).wait_recv()
+        loop(p, c + p, lambda i: forward_copy(2 * i + 1 - p).wait_recv())
 
     limit = jnp.where(h > 0, rows + keep * (h - 1), 0)
     bias = jnp.where(lax.broadcasted_iota(jnp.int32, (1, far), 1) < limit, 0.0, -jnp.inf)
@@ -248,23 +252,24 @@
     def _():
         second_half().wait_send()
         half_copy(0, far, 1).wait_send()
-        loop(1, n // 2, lambda i: half_copy(0, far, 2 * i).wait_send())
+        loop(1, chips, lambda i: half_copy(0, far, 2 * i).wait_send())
 
     @pl.when(h == 1)
     def _():
-        loop(1, n // 2, lambda i: half_copy(1, 0, 2 * i + 1).wait_send())
+        loop(1, chips, lambda i: half_copy(1, 0, 2 * i + 1).wait_send())
 
     @pl.when(h > 0)
     def _():
-        loop(h + 1, n, lambda j: kept_copy(h, j).wait_send())
-
-    @pl.when((h > 1) & (lax.rem(h, 2) == 0))
-    def _():
-        half_copy(0, 0, h + 1).wait_send()
-
-    @pl.when((h > 1) & (lax.rem(h, 2) == 1))
-    def _():
-        half_copy(1, 0, h - 1).wait_send()
+        loop(c + 1, chips, lambda i: kept_copy(h, 2 * i + p).wait_send())
+
+    @pl.when(c > 0)
+    def _():
+        @pl.when(p == 0)
+        def _():
+            kept_copy(h, h + 1).wait_send()
+
+        half_copy(p, 0, mate).wait_send()
+        loop(1 - p, c, lambda i: forward_copy(2 * i + p).wait_send())
 
     for step in range(len(order)):
         d = order[step][0]
@@ -302,6 +307,7 @@
             pltpu.SemaphoreType.DMA((n,)),
             pltpu.SemaphoreType.DMA((n,)),
             pltpu.SemaphoreType.DMA((n,)),
+            pltpu.SemaphoreType.DMA((n,)),
             pltpu.SemaphoreType.DMA((2,)),
             pltpu.SemaphoreType.DMA((tps * subs,)),
             pltpu.SemaphoreType.DMA((tps, subs)),

time: 17.4 us -> 16.8 us (0.966)
  the two profiles are of different devices: /device:TPU:28 before, /device:TPU:29 now
where the time goes in v4:
time: 16.8 us; the launch traced here: 16.7 us
  Pallas kernels  16 us (95%)
  local copies, waits for them, and re-layouts  0.71 us (4%)
    pallas_call x1, Pallas kernels, shards(): pl.pallas_call(functools.partial(kernel, n, tps, far, turn), out_shape=ja...  16 us
    unnamed x1, local copies, waits for them, and re-layouts  0.71 us

profile of v4, /device:TPU:29, one launch (start us, length us, event | category | flops | bytes accessed | tf_op | source)
XLA Modules:
  0.0 16.7 jit_solution(11545302492213560238)
XLA Ops:
  0.0 16.0 %shard_map.46 = bf16[64,2048]{1,0:T(8,128)(2,1)S(1)} custom-call(bf16[128,1024]{1,0:T(8,128)(2,1)} %q_hbm.1, bf16[128,128]{1,0:T(8,128)(2,1)} %k_hbm.1, bf16[128,128]{1,0:T(8,128)(2,1)} %v_hbm.1, s32[1,1,16]{2,1,0:T(1,128)} %pick_hbm.1), custom_call_target="tpu_custom_call" | custom-call | flops 268435456 | bytes 524288 | tf_op jit(solution)/shard_map/pallas_call | solution.py:293
  16.0 0.7 %copy.6 = bf16[64,2048]{1,0:T(8,128)(2,1)} copy(bf16[64,2048]{1,0:T(8,128)(2,1)S(1)} %shard_map.46) | data formatting | bytes 524288

commit v5 on v4

--- a/solution.py
+++ b/solution.py
@@ -15,7 +15,7 @@
 def kernel(
     n, tps, far, turn, q_hbm, k_hbm, v_hbm, pick_hbm, out,
     q, kv, kept, picks, local_scores, stage,
-    load_sem, ready, forward_send, kept_send, kept_recv, half_send, half_recv, out_send, out_recv, own_sem,
+    load_sem, forward_send, kept_send, kept_recv, half_send, half_recv, out_send, out_recv, own_sem,
 ):
     rows, width = q_hbm.shape
     hd = k_hbm.shape[1]
@@ -59,7 +59,7 @@
             barrier, inc=1, device_id={"tp": lax.rem(t + d, tps)}, device_id_type=MESH
         )
     greet(mate)
-    loop(c + 1, chips, lambda i: greet(2 * i + p))
+    loop(0, c, lambda i: greet(2 * i + p))
 
     def half_copy(side, base, j):
         return pltpu.make_async_remote_copy(
@@ -113,58 +113,6 @@
         preferred_element_type=jnp.float32,
     ).astype(kept.dtype)
 
-    pl.semaphore_wait(barrier, c + tps)
-
-    def tell(i):
-        pl.semaphore_signal(ready.at[h], inc=1, device_id={"ctx": 2 * i + p}, device_id_type=MESH)
-
-    loop(0, c, tell)
-
-    @pl.when(h == 0)
-    def _():
-        second_half().start()
-
-        def serve(i):
-            pl.semaphore_wait(ready.at[2 * i], 1)
-            half_copy(0, far, 2 * i).start()
-
-        loop(1, 2, serve)
-        half_copy(0, far, 1).start()
-        loop(2, chips, serve)
-
-    @pl.when(h == 1)
-    def _():
-        half_copy(1, 0, 0).wait_recv()
-
-        def serve(i):
-            pl.semaphore_wait(ready.at[2 * i + 1], 1)
-            half_copy(1, 0, 2 * i + 1).start()
-            kept_copy(1, 2 * i + 1).start()
-
-        loop(1, chips, serve)
-        half_copy(0, 0, 0).wait_recv()
-
-    @pl.when(c > 0)
-    def _():
-        @pl.when(p == 0)
-        def _():
-            kept_copy(h, h + 1).start()
-
-        def serve(i):
-            pl.semaphore_wait(ready.at[2 * i + p], 1)
-            kept_copy(h, 2 * i + p).start()
-
-        loop(c + 1, chips, serve)
-        half_copy(p, 0, 0).wait_recv()
-        half_copy(p, 0, mate).start()
-
-        def forward(i):
-            owner = 2 * i + p
-            forward_copy(owner).wait_recv()
-            forward_copy(owner).start()
-
-        loop(1 - p, c, forward)
-
     loads[3].wait()
     tall = group * turn
     contract = (((1,), (1,)), ((), ()))
@@ -190,6 +138,49 @@
             ),
             -jnp.inf,
         )
+
+    pl.semaphore_wait(barrier, chips - 1 - c + tps)
+
+    @pl.when(h == 0)
+    def _():
+        second_half().start()
+
+        def serve(i):
+            half_copy(0, far, 2 * i).start()
+
+        loop(1, 2, serve)
+        half_copy(0, far, 1).start()
+        loop(2, chips, serve)
+
+    @pl.when(h == 1)
+    def _():
+        half_copy(1, 0, 0).wait_recv()
+
+        def serve(i):
+            half_copy(1, 0, 2 * i + 1).start()
+            kept_copy(1, 2 * i + 1).start()
+
+        loop(1, chips, serve)
+        half_copy(0, 0, 0).wait_recv()
+
+    @pl.when(c > 0)
+    def _():
+        @pl.when(p == 0)
+        def _():
+            kept_copy(h, h + 1).start()
+
+        def serve(i):
+            kept_copy(h, 2 * i + p).start()
+
+        loop(c + 1, chips, serve)
+        def forward(i):
+            owner = 2 * i + p
+            forward_copy(owner).wait_recv()
+            forward_copy(owner).start()
+
+        loop(1 - p, c, forward)
+        half_copy(p, 0, 0).wait_recv()
+        half_copy(p, 0, mate).start()
 
     @pl.when(c > 0)
     def _():
@@ -303,7 +294,6 @@
             pltpu.VMEM((width // hd * rows, rows), jnp.float32),
             pltpu.VMEM((rows, width), jnp.bfloat16),
             pltpu.SemaphoreType.DMA((4,)),
-            pltpu.SemaphoreType.REGULAR((n,)),
             pltpu.SemaphoreType.DMA((n,)),
             pltpu.SemaphoreType.DMA((n,)),
             pltpu.SemaphoreType.DMA((n,)),

time: 16.8 us -> 18.5 us (1.10)
  the two profiles are of different devices: /device:TPU:29 before, /device:TPU:28 now
where the time goes in v5:
time: 18.5 us; the launch traced here: 18.4 us
  Pallas kernels  17.7 us (96%)
  local copies, waits for them, and re-layouts  0.71 us (4%)
    pallas_call x1, Pallas kernels, shards(): pl.pallas_call(functools.partial(kernel, n, tps, far, turn), out_shape=ja...  17.7 us
    unnamed x1, local copies, waits for them, and re-layouts  0.71 us

profile of v5, /device:TPU:28, one launch (start us, length us, event | category | flops | bytes accessed | tf_op | source)
XLA Modules:
  0.0 18.4 jit_solution(8312238251972916265)
XLA Ops:
  0.0 17.7 %shard_map.46 = bf16[64,2048]{1,0:T(8,128)(2,1)S(1)} custom-call(bf16[128,1024]{1,0:T(8,128)(2,1)} %q_hbm.1, bf16[128,128]{1,0:T(8,128)(2,1)} %k_hbm.1, bf16[128,128]{1,0:T(8,128)(2,1)} %v_hbm.1, s32[1,1,16]{2,1,0:T(1,128)} %pick_hbm.1), custom_call_target="tpu_custom_call" | custom-call | flops 268435456 | bytes 524288 | tf_op jit(solution)/shard_map/pallas_call | solution.py:284
  17.7 0.7 %copy.6 = bf16[64,2048]{1,0:T(8,128)(2,1)} copy(bf16[64,2048]{1,0:T(8,128)(2,1)S(1)} %shard_map.46) | data formatting | bytes 524288

commit v6 on v5

--- a/solution.py
+++ b/solution.py
@@ -15,7 +15,7 @@
 def kernel(
     n, tps, far, turn, q_hbm, k_hbm, v_hbm, pick_hbm, out,
     q, kv, kept, picks, local_scores, stage,
-    load_sem, forward_send, kept_send, kept_recv, half_send, half_recv, out_send, out_recv, own_sem,
+    load_sem, ready, forward_send, kept_send, kept_recv, half_send, half_recv, out_send, out_recv, own_sem,
 ):
     rows, width = q_hbm.shape
     hd = k_hbm.shape[1]
@@ -31,6 +31,24 @@
     mate = h + 1 - 2 * p
     scale = math.log2(math.e) / math.sqrt(hd)
 
+    barrier = pltpu.get_barrier_semaphore()
+
+    def loop(low, high, act):
+        def body(j, carry):
+            act(j)
+            return carry
+
+        lax.fori_loop(low, high, body, 0)
+
+    def greet(j):
+        pl.semaphore_signal(barrier, inc=1, device_id={"ctx": j}, device_id_type=MESH)
+
+    for d in range(1, tps):
+        pl.semaphore_signal(
+            barrier, inc=1, device_id={"tp": lax.rem(t + d, tps)}, device_id_type=MESH
+        )
+    loop(c + 1, chips, lambda i: greet(2 * i + p))
+
     loads = [
         pltpu.make_async_copy(k_hbm, kv.at[pl.ds(far, rows), pl.ds(0, hd)], load_sem.at[0]),
         pltpu.make_async_copy(v_hbm, kv.at[pl.ds(far, rows), pl.ds(hd, hd)], load_sem.at[1]),
@@ -42,24 +60,7 @@
     kv[0:far, 0 : 2 * hd] = jnp.zeros((far, 2 * hd), kv.dtype)
     kv[:, 2 * hd :] = jnp.ones((far + rows, hd), kv.dtype)
 
-    barrier = pltpu.get_barrier_semaphore()
-
-    def loop(low, high, act):
-        def body(j, carry):
-            act(j)
-            return carry
-
-        lax.fori_loop(low, high, body, 0)
-
-    def greet(j):
-        pl.semaphore_signal(barrier, inc=1, device_id={"ctx": j}, device_id_type=MESH)
-
-    for d in range(1, tps):
-        pl.semaphore_signal(
-            barrier, inc=1, device_id={"tp": lax.rem(t + d, tps)}, device_id_type=MESH
-        )
     greet(mate)
-    loop(0, c, lambda i: greet(2 * i + p))
 
     def half_copy(side, base, j):
         return pltpu.make_async_remote_copy(
@@ -113,6 +114,13 @@
         preferred_element_type=jnp.float32,
     ).astype(kept.dtype)
 
+    pl.semaphore_wait(barrier, c + tps)
+
+    def tell(i):
+        pl.semaphore_signal(ready.at[h], inc=1, device_id={"ctx": 2 * i + p}, device_id_type=MESH)
+
+    loop(0, c, tell)
+
     loads[3].wait()
     tall = group * turn
     contract = (((1,), (1,)), ((), ()))
@@ -139,13 +147,12 @@
             -jnp.inf,
         )
 
-    pl.semaphore_wait(barrier, chips - 1 - c + tps)
-
     @pl.when(h == 0)
     def _():
         second_half().start()
 
         def serve(i):
+            pl.semaphore_wait(ready.at[2 * i], 1)
             half_copy(0, far, 2 * i).start()
 
         loop(1, 2, serve)
@@ -157,6 +164,7 @@
         half_copy(1, 0, 0).wait_recv()
 
         def serve(i):
+            pl.semaphore_wait(ready.at[2 * i + 1], 1)
             half_copy(1, 0, 2 * i + 1).start()
             kept_copy(1, 2 * i + 1).start()
 
@@ -170,17 +178,19 @@
             kept_copy(h, h + 1).start()
 
         def serve(i):
+            pl.semaphore_wait(ready.at[2 * i + p], 1)
             kept_copy(h, 2 * i + p).start()
 
         loop(c + 1, chips, serve)
+        half_copy(p, 0, 0).wait_recv()
+        half_copy(p, 0, mate).start()
+
         def forward(i):
             owner = 2 * i + p
             forward_copy(owner).wait_recv()
             forward_copy(owner).start()
 
         loop(1 - p, c, forward)
-        half_copy(p, 0, 0).wait_recv()
-        half_copy(p, 0, mate).start()
 
     @pl.when(c > 0)
     def _():
@@ -294,6 +304,7 @@
             pltpu.VMEM((width // hd * rows, rows), jnp.float32),
             pltpu.VMEM((rows, width), jnp.bfloat16),
             pltpu.SemaphoreType.DMA((4,)),
+            pltpu.SemaphoreType.REGULAR((n,)),
             pltpu.SemaphoreType.DMA((n,)),
             pltpu.SemaphoreType.DMA((n,)),
             pltpu.SemaphoreType.DMA((n,)),

time: 18.5 us -> 16.6 us (0.90)
  the two profiles are of different devices: /device:TPU:28 before, /device:TPU:29 now
where the time goes in v6:
time: 16.6 us; the launch traced here: 16.4 us
  Pallas kernels  15.7 us (95%)
  local copies, waits for them, and re-layouts  0.71 us (4%)
    pallas_call x1, Pallas kernels, shards(): pl.pallas_call(functools.partial(kernel, n, tps, far, turn), out_shape=ja...  15.7 us
    unnamed x1, local copies, waits for them, and re-layouts  0.71 us

profile of v6, /device:TPU:29, one launch (start us, length us, event | category | flops | bytes accessed | tf_op | source)
XLA Modules:
  0.0 16.4 jit_solution(12147853302964814752)
XLA Ops:
  0.0 15.7 %shard_map.46 = bf16[64,2048]{1,0:T(8,128)(2,1)S(1)} custom-call(bf16[128,1024]{1,0:T(8,128)(2,1)} %q_hbm.1, bf16[128,128]{1,0:T(8,128)(2,1)} %k_hbm.1, bf16[128,128]{1,0:T(8,128)(2,1)} %v_hbm.1, s32[1,1,16]{2,1,0:T(1,128)} %pick_hbm.1), custom_call_target="tpu_custom_call" | custom-call | flops 268435456 | bytes 524288 | tf_op jit(solution)/shard_map/pallas_call | solution.py:294
  15.7 0.7 %copy.6 = bf16[64,2048]{1,0:T(8,128)(2,1)} copy(bf16[64,2048]{1,0:T(8,128)(2,1)S(1)} %shard_map.46) | data formatting | bytes 524288
